TPU v7x, 128 devices: a whole 4x4x4 slice. The times are simulated.
128 devices in a mesh: section: 2 (over x_hi), seq: 4 (over z), fsdp: 16 (over y, x_lo, core).
Axes of the slice: x: 4 (x_hi: 2, x_lo: 2; x = x_hi * 2 + x_lo), y: 4, z: 4, core: 2. Of those that a mesh axis runs over, the one named last changes fastest.
Arguments:
- images_in: bfloat16 [2, 16, 640, 768], P(None, 'fsdp', 'seq'), may hold values from -6 to 6
- counts: int32 [2, 16, 4], P(None, 'fsdp'), may hold values from 1 to 160, 577 in all within a row
- cotangent: bfloat16 [2, 16, 640, 768], P(None, 'fsdp', 'seq'), may hold values from -6 to 6
- gain_one: bfloat16 [2, 768], P('section', 'fsdp'), may hold values from 0.5 to 1.5
- shift_one: bfloat16 [2, 768], P('section', 'fsdp'), may hold values from -3 to 3
- w_qkv: bfloat16 [2, 768, 2304], P('section', 'fsdp'), may hold values from -0.21875 to 0.21875
- bias_query: bfloat16 [2, 768], P('section', 'fsdp'), may hold values from -3 to 3
- bias_value: bfloat16 [2, 768], P('section', 'fsdp'), may hold values from -3 to 3
- w_out: bfloat16 [2, 768, 768], P('section', 'fsdp'), may hold values from -3 to 3
- bias_out: bfloat16 [2, 768], P('section', 'fsdp'), may hold values from -3 to 3
- gain_two: bfloat16 [2, 768], P('section', 'fsdp'), may hold values from 0.5 to 1.5
- shift_two: bfloat16 [2, 768], P('section', 'fsdp'), may hold values from -3 to 3
- w_up: bfloat16 [2, 768, 3072], P('section', 'fsdp'), may hold values from -0.21875 to 0.21875
- bias_up: bfloat16 [2, 3072], P('section', 'fsdp'), may hold values from -3 to 3
- w_down: bfloat16 [2, 3072, 768], P('section', 'fsdp'), may hold values from -0.109375 to 0.109375
- bias_down: bfloat16 [2, 768], P('section', 'fsdp'), may hold values from -3 to 3
Outputs:
- layer_out: bfloat16 [2, 2, 16, 640, 768], P('section', None, 'fsdp', 'seq')
- input_grad: bfloat16 [2, 2, 16, 640, 768], P('section', None, 'fsdp', 'seq')
- grad_gain_one: float32 [2, 768], P('section', 'fsdp')
- grad_shift_one: float32 [2, 768], P('section', 'fsdp')
- grad_w_qkv: float32 [2, 768, 2304], P('section', 'fsdp')
- grad_bias_query: float32 [2, 768], P('section', 'fsdp')
- grad_bias_value: float32 [2, 768], P('section', 'fsdp')
- grad_w_out: float32 [2, 768, 768], P('section', 'fsdp')
- grad_bias_out: float32 [2, 768], P('section', 'fsdp')
- grad_gain_two: float32 [2, 768], P('section', 'fsdp')
- grad_shift_two: float32 [2, 768], P('section', 'fsdp')
- grad_w_up: float32 [2, 768, 3072], P('section', 'fsdp')
- grad_bias_up: float32 [2, 3072], P('section', 'fsdp')
- grad_w_down: float32 [2, 3072, 768], P('section', 'fsdp')
- grad_bias_down: float32 [2, 768], P('section', 'fsdp')
Inputs may be any that keep to these rules, and one draw needn't show every extreme that they name: For each image the 4 counts sum to 577 and at least one of them is 160; slots j < count of an index of seq hold live tokens, the others are padding.
All inputs are finite; a program needn't handle non-finite values.
Results may differ from a plain program's by a relative error of at most 0.019.
Values may be sent and summed in bfloat16 or wider, within the bound.
A program may use at most 256 MiB of HBM per device.

v0:
```python
import jax
import jax.numpy as jnp
from jax import lax
from jax.sharding import PartitionSpec as P

HD = 64


epsilon = 1e-06
masked_score = -1000000000.0


def sent_together(arrays, axis, dim, along):
    columns = [a.reshape(*a.shape[:along], -1) for a in arrays]
    both = jnp.concatenate(columns, axis=along)
    filled, at, outs = (lax.psum_scatter(both, axis, scatter_dimension=dim, tiled=True), 0, [])
    for a, column in zip(arrays, columns):
        piece = filled[..., at : at + column.shape[along]]
        outs.append(piece.reshape(*piece.shape[:along], *a.shape[along:]))
        at += column.shape[along]
    return tuple(outs)


def side_by_side(arrays, axis, dim, along):
    columns = [a.reshape(*a.shape[:along], -1) for a in arrays]
    both = jnp.concatenate(columns, axis=along)
    filled, at, outs = (lax.all_gather(both, axis, axis=dim, tiled=True), 0, [])
    for a, column in zip(arrays, columns):
        piece = filled[..., at : at + column.shape[along]]
        outs.append(piece.reshape(*piece.shape[:along], *a.shape[along:]))
        at += column.shape[along]
    return tuple(outs)


def passed_along(value, axis, steps):
    count = lax.axis_size(axis)
    leading, last = (max(0, -steps), min(count, count - steps))
    return lax.ppermute(value, axis, [(source, source + steps) for source in range(leading, last)])


def layer_norm(values, gain_vector, offset):
    average = jnp.mean(values, axis=-1, keepdims=True)
    centered = values - average
    spread = jnp.mean(centered * centered, axis=-1, keepdims=True)
    return centered * lax.rsqrt(spread + epsilon) * gain_vector + offset


def gelu_tanh(values):
    return jax.nn.gelu(values, approximate=True)


def contract_rows(left, right):
    return lax.dot_general(
        left, right, (((0,), (0,)), ((), ())), preferred_element_type=jnp.float32
    )


def contract_last(left, right):
    return lax.dot_general(
        left, right, (((1,), (1,)), ((), ())), preferred_element_type=jnp.float32
    )


def slot_masks(counts_now, seq_index, capacity):
    seq_count = counts_now.shape[1]
    chosen = lax.broadcasted_iota(jnp.int32, (1, seq_count), 1) == seq_index
    own_count = jnp.sum(jnp.where(chosen, counts_now, 0), axis=1)
    positions = lax.broadcasted_iota(jnp.int32, (1, capacity), 1)
    own_valid = (positions < own_count[:, None]).astype(jnp.float32)
    key_valid = (positions[:, None, :] < counts_now[:, :, None]).astype(jnp.float32)
    return (own_valid, key_valid.reshape(counts_now.shape[0], seq_count * capacity))


def split_heads(triples):
    slot_count, _, features = triples.shape
    shaped = triples.reshape(slot_count, 3, features // HD, HD)
    return (shaped[:, 0], shaped[:, 1], shaped[:, 2])


def masked_scores(query_side, key_side, key_valid):
    scores = jnp.einsum(
        "qhd,khd->hqk", query_side, key_side, preferred_element_type=jnp.float32
    ) * HD ** (-0.5)
    return jnp.where(key_valid[None, None, :] > 0, scores, masked_score)


def attend_image(packed):
    triples, key_valid = packed
    query_side, key_side, value_side = split_heads(triples)
    scores = masked_scores(query_side, key_side, key_valid)
    highest = jnp.max(scores, axis=-1, keepdims=True)
    raised = jnp.exp(scores - highest)
    totals = jnp.sum(raised, axis=-1, keepdims=True)
    weights_low = (raised / totals).astype(jnp.bfloat16)
    mixture = jnp.einsum(
        "hqk,khd->qhd", weights_low, value_side, preferred_element_type=jnp.float32
    )
    log_total = (highest + jnp.log(totals))[:, :, 0]
    return (mixture.reshape(triples.shape[0], triples.shape[2]).astype(jnp.bfloat16), log_total)


def attend_back(packed):
    triples, key_valid, log_total, grad_mixture = packed
    query_side, key_side, value_side = split_heads(triples)
    scores = masked_scores(query_side, key_side, key_valid)
    weights_soft = jnp.exp(scores - log_total[:, :, None])
    weights_low = weights_soft.astype(jnp.bfloat16)
    grad_shaped = grad_mixture.reshape(query_side.shape)
    grad_weights = jnp.einsum(
        "qhd,khd->hqk", grad_shaped, value_side, preferred_element_type=jnp.float32
    )
    grad_value = jnp.einsum(
        "hqk,qhd->khd", weights_low, grad_shaped, preferred_element_type=jnp.float32
    )
    row_inner = jnp.sum(weights_soft * grad_weights, axis=-1, keepdims=True)
    grad_scores = (weights_soft * (grad_weights - row_inner)).astype(jnp.bfloat16)
    grad_query = jnp.einsum(
        "hqk,khd->qhd", grad_scores, key_side, preferred_element_type=jnp.float32
    ) * HD ** (-0.5)
    grad_key = jnp.einsum(
        "hqk,qhd->khd", grad_scores, query_side, preferred_element_type=jnp.float32
    ) * HD ** (-0.5)
    stacked = jnp.stack([grad_query, grad_key, grad_value], axis=1)
    return stacked.reshape(triples.shape).astype(jnp.bfloat16)


def layer_forward(layer_input, own_valid, key_valid, weights):
    (
        gain_one,
        shift_one,
        w_qkv,
        bias_query,
        bias_value,
        w_out,
        bias_out,
        gain_two,
        shift_two,
        w_up,
        bias_up,
        w_down,
        bias_down,
    ) = weights
    images, capacity, features = layer_input.shape
    flat_rows = layer_input.astype(jnp.float32).reshape(images * capacity, features)
    normed = layer_norm(
        flat_rows, gain_one.astype(jnp.float32), shift_one.astype(jnp.float32)
    ).astype(jnp.bfloat16)
    bias_all = jnp.concatenate([bias_query, jnp.zeros_like(bias_query), bias_value]).astype(
        jnp.float32
    )
    triples = (jnp.dot(normed, w_qkv, preferred_element_type=jnp.float32) + bias_all).astype(
        jnp.bfloat16
    )
    triples = triples.reshape(images, capacity, 3, features)
    head_side = lax.all_to_all(triples, "seq", split_axis=3, concat_axis=1, tiled=True)
    attended, log_total = lax.map(attend_image, (head_side, key_valid))
    merged = lax.all_to_all(attended, "seq", split_axis=1, concat_axis=2, tiled=True).reshape(
        images * capacity, features
    )
    middle = (
        flat_rows
        + jnp.dot(merged, w_out, preferred_element_type=jnp.float32)
        + bias_out.astype(jnp.float32)
    )
    normed_two = layer_norm(
        middle, gain_two.astype(jnp.float32), shift_two.astype(jnp.float32)
    ).astype(jnp.bfloat16)
    hidden = jnp.dot(normed_two, w_up, preferred_element_type=jnp.float32) + bias_up.astype(
        jnp.float32
    )
    activated = gelu_tanh(hidden).astype(jnp.bfloat16)
    branch_two = jnp.dot(activated, w_down, preferred_element_type=jnp.float32) + bias_down.astype(
        jnp.float32
    )
    result = (middle + branch_two) * own_valid.reshape(images * capacity, 1)
    result = result.reshape(images, capacity, features).astype(jnp.bfloat16)
    return (
        result,
        (layer_input, own_valid, key_valid, head_side, log_total, merged, middle, hidden),
    )


def layer_backward(weights, stored, grad_result):
    (
        gain_one,
        shift_one,
        w_qkv,
        bias_query,
        bias_value,
        w_out,
        bias_out,
        gain_two,
        shift_two,
        w_up,
        bias_up,
        w_down,
        bias_down,
    ) = weights
    layer_input, own_valid, key_valid, head_side, log_total, merged, middle, hidden = stored
    images, capacity, features = layer_input.shape
    flat_rows = layer_input.astype(jnp.float32).reshape(images * capacity, features)
    grad_rows = grad_result.astype(jnp.float32).reshape(
        images * capacity, features
    ) * own_valid.reshape(images * capacity, 1)
    grad_down = grad_rows.astype(jnp.bfloat16)
    activated_full, gelu_pull = jax.vjp(gelu_tanh, hidden)
    activated = activated_full.astype(jnp.bfloat16)
    grad_w_down = contract_rows(activated, grad_down)
    grad_bias_down = jnp.sum(grad_down.astype(jnp.float32), axis=0)
    grad_hidden = gelu_pull(contract_last(grad_down, w_down))[0].astype(jnp.bfloat16)
    grad_bias_up = jnp.sum(grad_hidden.astype(jnp.float32), axis=0)
    normed_two_full, norm_two_pull = jax.vjp(
        layer_norm, middle, gain_two.astype(jnp.float32), shift_two.astype(jnp.float32)
    )
    grad_w_up = contract_rows(normed_two_full.astype(jnp.bfloat16), grad_hidden)
    grad_middle, grad_gain_two, grad_shift_two = norm_two_pull(contract_last(grad_hidden, w_up))
    grad_middle = grad_middle + grad_rows
    grad_branch = grad_middle.astype(jnp.bfloat16)
    grad_bias_out = jnp.sum(grad_branch.astype(jnp.float32), axis=0)
    grad_w_out = contract_rows(merged, grad_branch)
    grad_merged = (
        contract_last(grad_branch, w_out).astype(jnp.bfloat16).reshape(images, capacity, features)
    )
    grad_heads = lax.all_to_all(grad_merged, "seq", split_axis=2, concat_axis=1, tiled=True)
    grad_triples = lax.map(attend_back, (head_side, key_valid, log_total, grad_heads))
    grad_qkv = lax.all_to_all(grad_triples, "seq", split_axis=1, concat_axis=3, tiled=True).reshape(
        images * capacity, 3 * features
    )
    grad_bias_query = jnp.sum(grad_qkv[:, :features].astype(jnp.float32), axis=0)
    grad_bias_value = jnp.sum(grad_qkv[:, 2 * features :].astype(jnp.float32), axis=0)
    normed_full, norm_one_pull = jax.vjp(
        layer_norm, flat_rows, gain_one.astype(jnp.float32), shift_one.astype(jnp.float32)
    )
    grad_w_qkv = contract_rows(normed_full.astype(jnp.bfloat16), grad_qkv)
    grad_flat, grad_gain_one, grad_shift_one = norm_one_pull(contract_last(grad_qkv, w_qkv))
    grad_input = (grad_flat + grad_middle).reshape(images, capacity, features)
    gradients = (
        grad_gain_one,
        grad_shift_one,
        grad_w_qkv,
        grad_bias_query,
        grad_bias_value,
        grad_w_out,
        grad_bias_out,
        grad_gain_two,
        grad_shift_two,
        grad_w_up,
        grad_bias_up,
        grad_w_down,
        grad_bias_down,
    )
    return (grad_input, gradients)


def owner_shares(gradients):
    return (
        *tuple(
            (
                part.astype(jnp.float32)
                for part in sent_together(
                    (
                        gradients[0][None].astype(jnp.bfloat16),
                        gradients[1][None].astype(jnp.bfloat16),
                        gradients[2][None].astype(jnp.bfloat16),
                        gradients[3][None].astype(jnp.bfloat16),
                        gradients[4][None].astype(jnp.bfloat16),
                        gradients[5][None].astype(jnp.bfloat16),
                        gradients[6][None].astype(jnp.bfloat16),
                        gradients[7][None].astype(jnp.bfloat16),
                        gradients[8][None].astype(jnp.bfloat16),
                        gradients[9][None].astype(jnp.bfloat16),
                    ),
                    "fsdp",
                    1,
                    2,
                )
            )
        ),
        *tuple(
            (
                part.astype(jnp.float32)
                for part in sent_together(
                    (
                        gradients[10][None].astype(jnp.bfloat16),
                        gradients[11][None].astype(jnp.bfloat16),
                    ),
                    "fsdp",
                    1,
                    2,
                )
            )
        ),
        lax.psum_scatter(
            gradients[12][None].astype(jnp.bfloat16), "fsdp", scatter_dimension=1, tiled=True
        ).astype(jnp.float32),
    )


def per_device(
    images_in,
    counts,
    cotangent,
    gain_one,
    shift_one,
    w_qkv,
    bias_query,
    bias_value,
    w_out,
    bias_out,
    gain_two,
    shift_two,
    w_up,
    bias_up,
    w_down,
    bias_down,
):
    section_index = lax.axis_index("section")
    seq_index = lax.axis_index("seq")
    micro_count = images_in.shape[0]
    capacity = images_in.shape[2]
    gathered = (
        *side_by_side(
            (
                gain_one,
                shift_one,
                w_qkv,
                bias_query,
                bias_value,
                w_out,
                bias_out,
                gain_two,
                shift_two,
                w_up,
            ),
            "fsdp",
            1,
            2,
        ),
        *side_by_side((bias_up, w_down), "fsdp", 1, 2),
        lax.all_gather(bias_down, "fsdp", axis=1, tiled=True),
    )
    weights = tuple((member[0] for member in gathered))
    incoming = jnp.zeros(images_in.shape[1:], jnp.bfloat16)
    outputs = []
    stored_list = []
    for timestep in range(micro_count + 1):
        own_input = images_in[min(timestep, micro_count - 1)]
        layer_input = jnp.where(section_index == 0, own_input, incoming)
        batch_index = jnp.clip(timestep - section_index, 0, micro_count - 1)
        counts_now = lax.dynamic_index_in_dim(counts, batch_index, 0, keepdims=False)
        own_valid, key_valid = slot_masks(counts_now, seq_index, capacity)
        result, stored = layer_forward(layer_input, own_valid, key_valid, weights)
        outputs.append(result)
        stored_list.append(stored)
        if timestep < micro_count:
            incoming = passed_along(result, "section", 1)
    layer_out = lax.dynamic_slice_in_dim(jnp.stack(outputs), section_index, micro_count, 0)[None]
    stored_stack = jax.tree.map(lambda *members: jnp.stack(members), *stored_list)
    grad_incoming = jnp.zeros(images_in.shape[1:], jnp.bfloat16)
    back_outputs = []
    summed = None
    for timestep in range(micro_count + 1):
        if timestep < micro_count:
            own_grad = cotangent[timestep]
        else:
            own_grad = jnp.zeros_like(cotangent[0])
        grad_result = jnp.where(section_index == 1, own_grad, grad_incoming)
        forward_step = jnp.clip(timestep - 1 + 2 * section_index, 0, micro_count)
        stored = jax.tree.map(
            lambda member: lax.dynamic_index_in_dim(member, forward_step, 0, keepdims=False),
            stored_stack,
        )
        grad_input, gradients = layer_backward(weights, stored, grad_result)
        grad_low = grad_input.astype(jnp.bfloat16)
        back_outputs.append(grad_low)
        summed = gradients if summed is None else jax.tree.map(jnp.add, summed, gradients)
        if timestep < micro_count:
            grad_incoming = passed_along(grad_low, "section", -1)
    input_grad = lax.dynamic_slice_in_dim(
        jnp.stack(back_outputs), 1 - section_index, micro_count, 0
    )[None]
    shares = owner_shares(summed)
    totals = (
        lax.psum(shares[0].astype(jnp.bfloat16), "seq").astype(jnp.float32),
        lax.psum(shares[1].astype(jnp.bfloat16), "seq").astype(jnp.float32),
        lax.psum(shares[2].astype(jnp.bfloat16), "seq").astype(jnp.float32),
        lax.psum(shares[3].astype(jnp.bfloat16), "seq").astype(jnp.float32),
        lax.psum(shares[4].astype(jnp.bfloat16), "seq").astype(jnp.float32),
        lax.psum(shares[5].astype(jnp.bfloat16), "seq").astype(jnp.float32),
        lax.psum(shares[6].astype(jnp.bfloat16), "seq").astype(jnp.float32),
        lax.psum(shares[7].astype(jnp.bfloat16), "seq").astype(jnp.float32),
        lax.psum(shares[8].astype(jnp.bfloat16), "seq").astype(jnp.float32),
        lax.psum(shares[9].astype(jnp.bfloat16), "seq").astype(jnp.float32),
        lax.psum(shares[10].astype(jnp.bfloat16), "seq").astype(jnp.float32),
        lax.psum(shares[11].astype(jnp.bfloat16), "seq").astype(jnp.float32),
        lax.psum(shares[12].astype(jnp.bfloat16), "seq").astype(jnp.float32),
    )
    return (
        layer_out,
        input_grad,
        totals[0],
        totals[1],
        totals[2],
        totals[3],
        totals[4],
        totals[5],
        totals[6],
        totals[7],
        totals[8],
        totals[9],
        totals[10],
        totals[11],
        totals[12],
    )


def solution(mesh):
    placed = (
        P(None, "fsdp", "seq", None),
        P(None, "fsdp", None),
        P(None, "fsdp", "seq", None),
        P("section", "fsdp"),
        P("section", "fsdp"),
        P("section", "fsdp", None),
        P("section", "fsdp"),
        P("section", "fsdp"),
        P("section", "fsdp", None),
        P("section", "fsdp"),
        P("section", "fsdp"),
        P("section", "fsdp"),
        P("section", "fsdp", None),
        P("section", "fsdp"),
        P("section", "fsdp", None),
        P("section", "fsdp"),
    )
    return jax.shard_map(
        per_device,
        mesh=mesh,
        in_specs=placed,
        out_specs=(
            P("section", None, "fsdp", "seq", None),
            P("section", None, "fsdp", "seq", None),
            P("section", "fsdp"),
            P("section", "fsdp"),
            P("section", "fsdp", None),
            P("section", "fsdp"),
            P("section", "fsdp"),
            P("section", "fsdp", None),
            P("section", "fsdp"),
            P("section", "fsdp"),
            P("section", "fsdp"),
            P("section", "fsdp", None),
            P("section", "fsdp"),
            P("section", "fsdp", None),
            P("section", "fsdp"),
        ),
        check_vma=False,
    )
```

profile of v0, /device:TPU:0, one launch (start us, length us, event | category | flops | bytes accessed | tf_op | source)
XLA Modules:
  0.0 908.9 jit_solution(217611572123351840)
XLA Ops:
  18.0 57.4 %all-gather.3.cloned.1.call-done = bf16[1,768,6151]{2,1,0:T(8,128)(2,1)} async-done(((bf16[1,48,6151]{2,1,0:T(8,128)(2,1)}), bf16[1,768,6151]{2,1,0:T(8,128)(2,1)}) %all-gather.3.cloned.1.call-update) | async-done | bytes 9447952 | tf_op jit(solution)/shard_map/all_gather | solution.py:27
  94.7 10.3 %all-to-all-done = bf16[4,2,46080]{2,1,0:T(2,128)(2,1)S(1)} async-done(((bf16[4,2,46080]{2,1,0:T(2,128)(2,1)}), bf16[4,2,46080]{2,1,0:T(2,128)(2,1)S(1)}, u32[]{:S(2)}, u32[]{:S(2)}) %all-to-all-start) | async-done | bytes 737312 | tf_op jit(solution)/shard_map/all_to_all | solution.py:155
  126.0 29.1 %all-reduce = bf16[768]{0:T(1024)(128)(2,1)S(1)} all-reduce(bf16[768]{0:T(1024)(128)(2,1)S(1)} %dynamic-update-slice), channel_id=1, replica_groups=mesh['section'=2,'seq'=4,'fsdp'=16] {'fsdp'}, use_global_device_ids=true, to_apply=%add | all-reduce | flops 768 | bytes 3072
  185.1 5.2 all-to-all-start.2
  193.5 6.5 all-to-all-done.2
  238.3 5.9 collective-permute-start.1
  263.2 7.6 all-to-all-done.4
  344.8 4.9 all-to-all-start.6
  349.7 6.7 fusion.158
  388.8 5.0 all-to-all-start.7
  397.0 5.1 fusion.266
  418.5 7.8 collective-permute-done.2
  427.0 6.9 convert_reduce_fusion.1
  478.1 6.7 fusion.156
  484.8 5.2 all-to-all-done.9
  502.8 5.4 collective-permute-done.3
  508.3 7.2 convert_reduce_fusion
  515.7 5.7 fusion.1
  521.4 5.7 pad_maximum_fusion.1
  527.1 23.7 %copy.366 = bf16[1,3072,769]{2,0,1:T(2,128)(2,1)} copy(bf16[1,3072,769]{1,2,0:T(8,128)(2,1)} %pad_maximum_fusion.1) | data formatting | bytes 9449472
  550.8 7.4 copy.377
  559.6 6.5 fusion.267
  566.2 5.2 fusion.271
  615.9 4.9 all-to-all-start.11
  621.0 10.3 %fusion = bf16[1,768,3072]{2,1,0:T(8,128)(2,1)} fusion(bf16[160,3072]{1,0:T(8,128)(2,1)S(1)} %copy-done.59, f32[768,3072]{1,0:T(8,128)} %fusion.266, f32[768,3072]{1,0:T(8,128)} %fusion.267, f32[3,160,768]{2,1,0:T(8,128)S(1)} %copy-done.1, s32[]{:T(128)S(6)} %min.24, f32[160]{0:T(256)S(1)} %fusion.375, f32[160]{0:T(256)S(1)} %copy-done.121, ...), kind=kOutput, calls=%fused_computation.26 | convolution fusion | flops 762667008 | bytes 25077764 | tf_op jit(solution)/shard_map/dot_general | solution.py:53
  647.7 6.0 fusion.2
  653.7 21.0 %concatenate.60 = bf16[1,768,6151]{2,1,0:T(8,128)(2,1)} concatenate(bf16[1,768,1]{2,1,0:T(8,128)(2,1)} %convert_element_type.987, bf16[1,768,1]{2,1,0:T(8,128)(2,1)} %convert_element_type.988, bf16[1,768,2304]{2,1,0:T(8,128)(2,1)} %fusion.2, bf16[1,768,1]{2,1,0:T(8,128)(2,1)} %convert_element_type.989, bf16[1,768,1]{2,1,0:T(8,128)(2,1)} %convert_element_type.990, ...), dimensions={2} | concatenate | bytes 18895872 | tf_op jit(solution)/shard_map/concatenate | solution.py:15
  683.0 102.2 %reduce-scatter.8.cloned.1.call-done = bf16[1,48,6151]{2,1,0:T(8,128)(2,1)} async-done(((bf16[1,768,6151]{2,1,0:T(8,128)(2,1)}), bf16[1,48,6151]{2,1,0:T(8,128)(2,1)}) %reduce-scatter.8.cloned.1.call-update) | async-done | bytes 590512 | tf_op jit(solution)/shard_map/reduce_scatter | solution.py:16
  790.6 5.0 fusion.148
  797.7 48.7 %reduce-scatter.12.cloned.1.call-done = bf16[48,1]{1,0:T(8,128)(2,1)} async-done(((bf16[768,1]{1,0:T(8,128)(2,1)}), bf16[48,1]{1,0:T(8,128)(2,1)}) %reduce-scatter.12.cloned.1.call-update) | async-done | bytes 112
  848.7 10.8 %all-reduce.1 = (bf16[1,48]{1,0:T(2,128)(2,1)S(1)}, bf16[1,48]{1,0:T(2,128)(2,1)S(1)}, bf16[1,48]{1,0:T(2,128)(2,1)S(1)}, bf16[1,48]{1,0:T(2,128)(2,1)S(1)}, bf1...) all-reduce(bf16[1,48]{1,0:T(2,128)(2,1)S(1)} %bitcast.827, ...), channel_id=1, replica_groups=mesh['section'=2,'seq'=4,'fsdp'=16] {'seq'}, use_global_device_ids=true, to_apply=%region_70.71 | all-reduce | flops 576 | bytes 2304 | tf_op jit(solution)/shard_map/psum | solution.py:384
  864.1 30.6 %all-reduce.5.cloned.1.call-done = (bf16[1,192,768]{1,2,0:T(8,128)(2,1)}, bf16[1,48,2304]{2,1,0:T(8,128)(2,1)}, bf16[1,48,768]{2,1,0:T(8,128)(2,1)}, bf16[1,48,3072]{2,1,0:T(8,128)(2,1)}) async-done(((bf16[1,192,768]{1,2,0:T(8,128)(2,1)}, bf16[1,48,2304]{2,1,0:T(8,128)(2,1)}, bf16[1,48,768]{2,1,0:T(8,128)(2,1)}, bf16[1,48,3072]{2,1,0:T(8,128)(2,1)}), (bf16[1,192,768]{1,2,0:T(8,128)(2,1)}, ...) | async-done | bytes 884752 | tf_op jit(solution)/shard_map/psum | solution.py:395
  (707 shorter events, 413.9 us)
Async XLA Ops:
  7.2 68.2 %all-gather.3.cloned.1.call-start = ((), (), s32[]{:S(2)}) async-start(), calls=%async_computation.15 | async-start | bytes 10235904 | tf_op jit(solution)/shard_map/all_gather | solution.py:27
  14.8 140.3 %all-gather.5.cloned.1.call-start = ((), (), s32[]{:S(2)}) async-start(), calls=%async_computation.16 | async-start | bytes 5849088 | tf_op jit(solution)/shard_map/all_gather | solution.py:27
  17.8 139.9 %copy-start.25 = (bf16[1,1,160,768]{3,2,1,0:T(8,128)(2,1)}, bf16[1,1,160,768]{3,2,1,0:T(8,128)(2,1)S(1)}, u32[]{:S(2)}) copy-start(bf16[1,1,160,768]{3,2,1,0:T(8,128)(2,1)S(1)} %get-tuple-element.279) | copy-start | bytes 737284
  88.2 16.7 %all-to-all-start = ((bf16[4,2,46080]{2,1,0:T(2,128)(2,1)}), bf16[4,2,46080]{2,1,0:T(2,128)(2,1)S(1)}, u32[]{:S(2)}, u32[]{:S(2)}) async-start(bf16[4,2,46080]{2,1,0:T(2,128)(2,1)} %reshape.1675), calls=%async_computation | async-start | bytes 1474560 | tf_op jit(solution)/shard_map/all_to_all | solution.py:155
  119.4 38.3 %copy-start.127 = (f32[768]{0:T(1024)S(1)}, f32[768]{0:T(1024)}, u32[]{:S(2)}) copy-start(f32[768]{0:T(1024)} %get-tuple-element.191) | copy-start | bytes 9220
  120.5 36.1 %all-to-all-start.1 = ((bf16[4,2,15360]{2,1,0:T(2,128)(2,1)}), bf16[4,2,15360]{2,1,0:T(2,128)(2,1)S(1)}, u32[]{:S(2)}, u32[]{:S(2)}) async-start(bf16[4,2,15360]{2,1,0:T(2,128)(2,1)} %reshape.1677), calls=%async_computation.1 | async-start | bytes 491520 | tf_op jit(solution)/shard_map/all_to_all | solution.py:157
  167.0 8.4 collective-permute-start
  185.1 14.9 %all-to-all-start.2 = ((bf16[4,2,46080]{2,1,0:T(2,128)(2,1)}), bf16[4,2,46080]{2,1,0:T(2,128)(2,1)S(1)}, u32[]{:S(2)}, u32[]{:S(2)}) async-start(bf16[4,2,46080]{2,1,0:T(2,128)(2,1)} %reshape.1679), calls=%async_computation.2 | async-start | bytes 1474560 | tf_op jit(solution)/shard_map/all_to_all | solution.py:155
  217.8 10.1 %all-to-all-start.3 = ((bf16[4,2,15360]{2,1,0:T(2,128)(2,1)}), bf16[4,2,15360]{2,1,0:T(2,128)(2,1)S(1)}, u32[]{:S(2)}, u32[]{:S(2)}) async-start(bf16[4,2,15360]{2,1,0:T(2,128)(2,1)} %reshape.1681), calls=%async_computation.3 | async-start | bytes 491520 | tf_op jit(solution)/shard_map/all_to_all | solution.py:157
  238.3 9.6 %collective-permute-start.1 = (bf16[1,160,768]{2,1,0:T(8,128)(2,1)S(1)}, bf16[1,160,768]{2,1,0:T(8,128)(2,1)S(1)}, u32[]{:S(2)}, u32[]{:S(2)}) collective-permute-start(bf16[1,160,768]{2,1,0:T(8,128)(2,1)S(1)} %bitcast.786), channel_id=1, source_target_pairs={{0,64},{1,65},{2,66},{3,67},{4,68},{5,69},{6,70},{7,71},{8,72},{9,... | collective-permute-start | bytes 737288 | tf_op jit(solution)/shard_map/ppermute | solution.py:38
  258.0 12.9 %all-to-all-start.4 = ((bf16[4,2,46080]{2,1,0:T(2,128)(2,1)}), bf16[4,2,46080]{2,1,0:T(2,128)(2,1)S(1)}, u32[]{:S(2)}, u32[]{:S(2)}) async-start(bf16[4,2,46080]{2,1,0:T(2,128)(2,1)} %reshape.1683), calls=%async_computation.4 | async-start | bytes 1474560 | tf_op jit(solution)/shard_map/all_to_all | solution.py:155
  261.8 186.2 %copy-start.4 = (bf16[3,1,160,768]{3,2,1,0:T(8,128)(2,1)}, bf16[3,1,160,768]{3,2,1,0:T(8,128)(2,1)S(1)}, u32[]{:S(2)}) copy-start(bf16[3,1,160,768]{3,2,1,0:T(8,128)(2,1)S(1)} %pad_maximum_fusion.7) | copy-start | bytes 2211844
  290.2 21.1 %all-to-all-start.5 = ((bf16[4,2,15360]{2,1,0:T(2,128)(2,1)}), bf16[4,2,15360]{2,1,0:T(2,128)(2,1)S(1)}, u32[]{:S(2)}, u32[]{:S(2)}) async-start(bf16[4,2,15360]{2,1,0:T(2,128)(2,1)} %reshape.1685), calls=%async_computation.5 | async-start | bytes 491520 | tf_op jit(solution)/shard_map/all_to_all | solution.py:157
  316.1 120.8 %copy-start = (f32[3,160,768]{2,1,0:T(8,128)}, f32[3,160,768]{2,1,0:T(8,128)S(1)}, u32[]{:S(2)}) copy-start(f32[3,160,768]{2,1,0:T(8,128)S(1)} %pad_maximum_fusion.3) | copy-start | bytes 4423684
  344.8 14.4 %all-to-all-start.6 = ((bf16[4,2,15360]{2,1,0:T(2,128)(2,1)}), bf16[4,2,15360]{2,1,0:T(2,128)(2,1)}, u32[]{:S(2)}, u32[]{:S(2)}) async-start(bf16[4,2,15360]{2,1,0:T(2,128)(2,1)} %reshape.1687), calls=%async_computation.6 | async-start | bytes 491520 | tf_op jit(solution)/shard_map/all_to_all | solution.py:224
  388.8 17.3 %all-to-all-start.7 = ((bf16[1,640,3,192]{3,2,0,1:T(4,128)(2,1)}), bf16[1,640,3,192]{3,2,0,1:T(4,128)(2,1)S(1)}, u32[]{:S(2)}, u32[]{:S(2)}) async-start(bf16[1,640,3,192]{3,2,0,1:T(4,128)(2,1)} %pad_maximum_fusion.4), calls=%async_computation.7 | async-start | bytes 2621440 | tf_op jit(solution)/shard_map/all_to_all | solution.py:226
  410.3 23.6 %slice-start.17 = ((s8[9633792]{0:T(1024)(128)(4,1)}), s8[4194304]{0:T(1024)(128)(4,1)S(1)}, s32[]{:S(2)}) async-start(s8[9633792]{0:T(1024)(128)(4,1)} %bitcast.796), calls=%async_computation.38 | async-start | bytes 8388608
  416.6 9.7 %collective-permute-start.2 = (bf16[1,160,768]{2,1,0:T(8,128)(2,1)S(1)}, bf16[1,160,768]{2,1,0:T(8,128)(2,1)S(1)}, u32[]{:S(2)}, u32[]{:S(2)}) collective-permute-start(bf16[1,160,768]{2,1,0:T(8,128)(2,1)S(1)} %bitcast.776), channel_id=1, source_target_pairs={{64,0},{65,1},{66,2},{67,3},{68,4},{69,5},{70,6},{71,7},{72,8},{73... | collective-permute-start | bytes 737288 | tf_op jit(solution)/shard_map/ppermute | solution.py:38
  444.4 10.1 %all-to-all-start.8 = ((bf16[4,2,15360]{2,1,0:T(2,128)(2,1)}), bf16[4,2,15360]{2,1,0:T(2,128)(2,1)S(1)}, u32[]{:S(2)}, u32[]{:S(2)}) async-start(bf16[4,2,15360]{2,1,0:T(2,128)(2,1)} %reshape.1689), calls=%async_computation.8 | async-start | bytes 491520 | tf_op jit(solution)/shard_map/all_to_all | solution.py:224
  474.2 15.8 %all-to-all-start.9 = ((bf16[1,640,3,192]{3,2,0,1:T(4,128)(2,1)}), bf16[1,640,3,192]{3,2,0,1:T(4,128)(2,1)S(1)}, u32[]{:S(2)}, u32[]{:S(2)}) async-start(bf16[1,640,3,192]{3,2,0,1:T(4,128)(2,1)} %pad_maximum_fusion.5), calls=%async_computation.9 | async-start | bytes 2621440 | tf_op jit(solution)/shard_map/all_to_all | solution.py:226
  477.7 201.3 %reduce-scatter.10.cloned.1.call-start = ((), (), s32[]{:S(2)}) async-start(), calls=%async_computation.18 | async-start | bytes 5849088
  490.0 25.6 %slice-start.3 = ((s8[9437184]{0:T(1024)(128)(4,1)}), s8[1048576]{0:T(1024)(128)(4,1)S(1)}, s32[]{:S(2)}) async-start(s8[9437184]{0:T(1024)(128)(4,1)} %bitcast.706), calls=%async_computation.24 | async-start | bytes 2097152
  498.6 9.6 %collective-permute-start.3 = (bf16[1,160,768]{2,1,0:T(8,128)(2,1)S(1)}, bf16[1,160,768]{2,1,0:T(8,128)(2,1)S(1)}, u32[]{:S(2)}, u32[]{:S(2)}) collective-permute-start(bf16[1,160,768]{2,1,0:T(8,128)(2,1)S(1)} %bitcast.774), channel_id=1, source_target_pairs={{64,0},{65,1},{66,2},{67,3},{68,4},{69,5},{70,6},{71,7},{72,8},{73... | collective-permute-start | bytes 737288 | tf_op jit(solution)/shard_map/ppermute | solution.py:38
  508.2 65.6 %copy-start.31 = (bf16[1,160,768]{2,1,0:T(8,128)(2,1)}, bf16[1,160,768]{2,1,0:T(8,128)(2,1)S(1)}, u32[]{:S(2)}) copy-start(bf16[1,160,768]{2,1,0:T(8,128)(2,1)S(1)} %collective-permute-done.3) | copy-start | bytes 737284
  580.5 10.8 %all-to-all-start.10 = ((bf16[4,2,15360]{2,1,0:T(2,128)(2,1)}), bf16[4,2,15360]{2,1,0:T(2,128)(2,1)S(1)}, u32[]{:S(2)}, u32[]{:S(2)}) async-start(bf16[4,2,15360]{2,1,0:T(2,128)(2,1)} %reshape.1691), calls=%async_computation.10 | async-start | bytes 491520 | tf_op jit(solution)/shard_map/all_to_all | solution.py:224
  615.9 17.3 %all-to-all-start.11 = ((bf16[1,640,3,192]{3,2,0,1:T(4,128)(2,1)}), bf16[1,640,3,192]{3,2,0,1:T(4,128)(2,1)}, u32[]{:S(2)}, u32[]{:S(2)}) async-start(bf16[1,640,3,192]{3,2,0,1:T(4,128)(2,1)} %pad_maximum_fusion.6), calls=%async_computation.11 | async-start | bytes 2621440 | tf_op jit(solution)/shard_map/all_to_all | solution.py:226
  620.8 164.4 %reduce-scatter.8.cloned.1.call-start = ((), (), s32[]{:S(2)}) async-start(), calls=%async_computation.17 | async-start | bytes 10235904 | tf_op jit(solution)/shard_map/reduce_scatter | solution.py:16
  674.8 171.7 %reduce-scatter.12.cloned.1.call-start = ((), (), s32[]{:S(2)}) async-start(), calls=%async_computation.19 | async-start | bytes 208896
  678.7 111.8 %copy-start.36 = (f32[160,3072]{1,0:T(8,128)S(1)}, f32[160,3072]{1,0:T(8,128)}, u32[]{:S(2)}) copy-start(f32[160,3072]{1,0:T(8,128)} %copy-done.35) | copy-start | bytes 5898244
  678.7 111.8 %copy-start.140 = (f32[768]{0:T(1024)S(1)}, f32[768]{0:T(1024)}, u32[]{:S(2)}) copy-start(f32[768]{0:T(1024)} %copy-done.138) | copy-start | bytes 9220
  678.7 111.8 %copy-start.142 = (f32[160]{0:T(256)S(1)}, f32[160]{0:T(256)}, u32[]{:S(2)}) copy-start(f32[160]{0:T(256)} %get-tuple-element.338) | copy-start | bytes 1924
  678.7 216.0 %all-reduce.5.cloned.1.call-start = ((), (), s32[]{:S(2)}) async-start(), calls=%async_computation.20 | async-start | bytes 1966080 | tf_op jit(solution)/shard_map/psum | solution.py:395
  (165 other events, 1065.5 us)
Sparse Core Ops, SparseCore 0:
  15.0 60.4 all-gather.2
  77.7 40.8 all-gather.4
  558.3 72.7 reduce-scatter.9
  674.9 110.2 reduce-scatter.7
  787.4 58.9 reduce-scatter.11
  850.3 44.4 all-reduce.4
where the time goes:
time: 917 us; the launch traced here: 909 us
  waiting for transfers between devices  297 us (32%)
  local copies, waits for them, and re-layouts  203 us (22%)
  matrix products  197 us (21%)
  other arithmetic  89.9 us (10%)
  starting transfers between devices  64.1 us (7%)
  blocking collectives  39.8 us (4%)
  between operations  18.1 us (2%)
    reduce_scatter x1, waiting for transfers between devices, sent_together(): lax.psum_scatter(both, axis, scatter_dimension=dim, tiled=True)  102 us
    unnamed x384, local copies, waits for them, and re-layouts  78.7 us
    dot_general x12, matrix products, contract_rows(): lax.dot_general(left, right, (((0,), (0,)), ((), ())), preferred_element_...  65.3 us
    all_gather x2, waiting for transfers between devices, side_by_side(): filled, at, outs = (lax.all_gather(both, axis, axis=dim, tiled=True), 0, [])  57.4 us
    unnamed x8, waiting for transfers between devices  48.8 us
    dot_general x12, matrix products, contract_last(): lax.dot_general(left, right, (((1,), (1,)), ((), ())), preferred_element_...  42.1 us
    psum x1, waiting for transfers between devices, per_device(): lax.psum(shares[11].astype(jnp.bfloat16), 'seq').astype(jnp.float32)  30.6 us
    unnamed x1, blocking collectives  29.1 us
  transfers between devices with their start and end apart: 22, of which 16 were waited for; matrix products, arithmetic and copies ran while one was open for 25% of the time, Pallas kernels for 0%

commit v1 on v0

v1 whole, which is shorter than its diff:
```python
import functools

import jax
import jax.numpy as jnp
from jax import lax
from jax.experimental import pallas as pl
from jax.experimental.pallas import tpu as pltpu
from jax.sharding import PartitionSpec as P

HD = 64
epsilon = 1e-06
masked_score = -1000000000.0
MESH = pl.DeviceIdType.MESH
bf16 = jnp.bfloat16
f32 = jnp.float32
VMEM_LIMIT = 56 * 1024 * 1024


def nn(a, b):
    return jnp.dot(a, b, preferred_element_type=f32)


def nt(a, b):
    return lax.dot_general(a, b, (((1,), (1,)), ((), ())), preferred_element_type=f32)


def tn(a, b):
    return lax.dot_general(a, b, (((0,), (0,)), ((), ())), preferred_element_type=f32)


def norm_parts(values):
    average = jnp.mean(values, axis=-1, keepdims=True)
    centered = values - average
    spread = jnp.mean(centered * centered, axis=-1, keepdims=True)
    inverse = lax.rsqrt(spread + epsilon)
    return centered * inverse, inverse


def norm_back(incoming, gain, xhat, inverse):
    e = incoming * gain
    inner = jnp.mean(e * xhat, axis=-1, keepdims=True)
    return (e - jnp.mean(e, axis=-1, keepdims=True) - xhat * inner) * inverse


def gelu_both(v):
    c = 0.7978845608028654
    square = v * v
    t = jnp.tanh(c * v * (1.0 + 0.044715 * square))
    half = 0.5 * (1.0 + t)
    slope = half + 0.5 * v * (1.0 - t * t) * (c * (1.0 + 0.134145 * square))
    return v * half, slope


def row_valid(counts, batch, cap, index):
    pos = lax.broadcasted_iota(jnp.int32, (cap, 1), 0)
    return jnp.concatenate([pos < counts[b, index] for b in range(batch)], axis=0)


def key_valid(counts, b, cap, sources):
    pos = lax.broadcasted_iota(jnp.int32, (cap, 1), 0)
    return jnp.concatenate([pos < counts[b, s] for s in sources], axis=0)


def greet(axis_ids):
    barrier = pltpu.get_barrier_semaphore()
    for ids in axis_ids:
        pl.semaphore_signal(barrier, inc=1, device_id=ids, device_id_type=MESH)
    pl.semaphore_wait(barrier, len(axis_ids))


def remote(src, dst, ssem, rsem, ids):
    return pltpu.make_async_remote_copy(
        src_ref=src, dst_ref=dst, send_sem=ssem, recv_sem=rsem, device_id=ids, device_id_type=MESH
    )


def load_weights(shards, wq_h, wo_h, wu_h, wd_h, wq, wo, wu, wd, sems, order):
    def start_q():
        rows = wq_h.shape[2]
        for f in range(shards):
            pltpu.make_async_copy(
                wq_h.at[f], wq.at[:, pl.ds(f * rows, rows), :], sems.at[0]
            ).start()

    starts = {
        "q": start_q,
        "o": lambda: pltpu.make_async_copy(wo_h, wo, sems.at[1]).start(),
        "u": lambda: pltpu.make_async_copy(wu_h, wu, sems.at[2]).start(),
        "d": lambda: pltpu.make_async_copy(wd_h, wd, sems.at[3]).start(),
    }
    for name in order:
        starts[name]()

    def wait(name):
        i, ref = {"q": (0, wq), "o": (1, wo), "u": (2, wu), "d": (3, wd)}[name]
        pltpu.make_async_copy(ref, ref, sems.at[i]).wait()

    return wait


def forward_kernel(
    shape,
    counts, own, got, gain1, shift1, bqkv, bo, gain2, shift2, bu, bd, wq_h, wo_h, wu_h, wd_h,
    y_out, next_out, qkv_out, lse_out, normed_out, mid_out, merged_out, n2_out, act_out, slope_out,
    wq, wo, wu, wd, sendq, recvq, senda, recva, land, wsem, sq, rq, sa, ra, ss, rs,
):
    batch, cap, seqs, shards, chunks = shape
    rows = batch * cap
    me = lax.axis_index("seq")
    sec = lax.axis_index("section")
    ahead = [lax.rem(me + d, seqs) for d in range(seqs)]
    behind = [lax.rem(me + seqs - d, seqs) for d in range(seqs)]
    peers = [{"seq": ahead[d]} for d in range(1, seqs)] + [{"section": 1 - sec}]
    wait_weight = load_weights(
        shards, wq_h, wo_h, wu_h, wd_h, wq, wo, wu, wd, wsem, ("q", "o", "u", "d")
    )
    x = jnp.where(sec == 0, own[...], got[...]).astype(f32)
    xhat, _ = norm_parts(x)
    normed = (xhat * gain1[...].astype(f32) + shift1[...].astype(f32)).astype(bf16)
    normed_out[...] = normed
    greet(peers)
    wait_weight("q")
    copies = []
    for d in list(range(1, seqs)) + [0]:
        t = ahead[d]
        res = (nn(normed_out[...], wq[t]) + bqkv[t].astype(f32)).astype(bf16)
        res = res.reshape(batch, cap, res.shape[-1])
        if d == 0:
            recvq[0] = res
        else:
            sendq[d - 1] = res
            copy = remote(sendq.at[d - 1], recvq.at[d], sq.at[d - 1], rq.at[d - 1], {"seq": t})
            copy.start()
            copies.append(copy)
    for copy in copies:
        copy.wait()
    keep = pltpu.make_async_copy(recvq, qkv_out, wsem.at[4])
    keep.start()
    width = recvq.shape[-1] // 3
    heads = width // HD
    lane = lax.broadcasted_iota(jnp.int32, (1, width), 1) // HD
    back = []
    for b in range(batch):
        qkv = recvq[:, b].reshape(seqs * cap, 3 * width)
        q, k, v = (qkv[:, i * width : (i + 1) * width] for i in range(3))
        q = q * jnp.asarray(HD ** (-0.5), bf16)
        vt = v.T
        live = key_valid(counts, b, cap, behind)
        outs = []
        for h in range(heads):
            qm = jnp.where(lane == h, q, jnp.zeros_like(q))
            s = jnp.where(live, nt(k, qm), masked_score)
            highest = jnp.max(s, axis=0, keepdims=True)
            raised = jnp.exp(s - highest)
            total = jnp.sum(raised, axis=0, keepdims=True)
            p = (raised * (1.0 / total)).astype(bf16)
            outs.append(nn(vt[h * HD : (h + 1) * HD], p))
            lse_out[b, h : h + 1, :] = highest + jnp.log(total)
        o = jnp.concatenate(outs, axis=0).T.astype(bf16).reshape(seqs, cap, width)
        recva[0, b] = o[0]
        for d in range(1, seqs):
            senda[d - 1, b] = o[d]
            copy = remote(
                senda.at[d - 1, b], recva.at[d, b], sa.at[d - 1, b], ra.at[d - 1, b], {"seq": behind[d]}
            )
            copy.start()
            back.append(copy)
    wait_weight("o")
    mid = jnp.where(sec == 0, own[...], got[...]).astype(f32) + bo[...].astype(f32)
    for copy in back:
        copy.wait()
    for d in range(seqs):
        part = recva[d].reshape(rows, width)
        merged_out[ahead[d]] = part
        mid = mid + nn(part, wo[ahead[d]])
    mid_out[...] = mid
    xhat2, _ = norm_parts(mid)
    n2_out[...] = (xhat2 * gain2[...].astype(f32) + shift2[...].astype(f32)).astype(bf16)
    wait_weight("u")
    wait_weight("d")
    total = None
    size = wu.shape[1] // chunks
    for c in range(chunks):
        part = slice(c * size, (c + 1) * size)
        hidden = nn(n2_out[...], wu[:, part]) + bu[:, part].astype(f32)
        activated, slope = gelu_both(hidden)
        activated = activated.astype(bf16)
        act_out[:, part] = activated
        slope_out[:, part] = slope.astype(bf16)
        term = nn(activated, wd[part])
        total = term if total is None else total + term
    live_rows = row_valid(counts, batch, cap, me)
    y = mid_out[...] + (total + bd[...].astype(f32))
    y_out[...] = jnp.where(live_rows, y, 0.0).astype(bf16)
    hop = remote(y_out, land, ss, rs, {"section": 1 - sec})
    hop.start()
    hop.wait()
    next_out[...] = land[...]
    keep.wait()


def backward_kernel(
    shape,
    counts, own, got, cot, ggot, lse, normed, mid, act, slope, gain1, gain2, qkv_h, wq_h, wo_h, wu_h, wd_h,
    dx_out, next_out, ddown_out, dhid_out, dbranch_out, dqkv_out, dgain1, dshift1, dbqkv, dbo, dgain2, dshift2, dbu, dbd,
    wq, wo, wu, wd, qkv, senda, recva, sendq, recvq, land, dmid, wsem, sa, ra, sq, rq, ss, rs,
):
    batch, cap, seqs, shards, chunks = shape
    rows = batch * cap
    me = lax.axis_index("seq")
    sec = lax.axis_index("section")
    ahead = [lax.rem(me + d, seqs) for d in range(seqs)]
    behind = [lax.rem(me + seqs - d, seqs) for d in range(seqs)]
    peers = [{"seq": ahead[d]} for d in range(1, seqs)] + [{"section": 1 - sec}]
    wait_weight = load_weights(
        shards, wq_h, wo_h, wu_h, wd_h, wq, wo, wu, wd, wsem, ("d", "u", "o", "q")
    )
    fetch = pltpu.make_async_copy(qkv_h, qkv, wsem.at[4])
    fetch.start()
    live_rows = row_valid(counts, batch, cap, me)
    g = jnp.where(sec == 0, ggot[...], cot[...])
    ddown_out[...] = jnp.where(live_rows, g.astype(f32), 0.0).astype(bf16)
    greet(peers)
    wait_weight("d")
    wait_weight("u")
    h2 = None
    size = wu.shape[1] // chunks
    for c in range(chunks):
        part = slice(c * size, (c + 1) * size)
        da = nt(ddown_out[...], wd[part])
        dh = (da * slope[:, part].astype(f32)).astype(bf16)
        dhid_out[:, part] = dh
        term = nt(dh, wu[:, part])
        h2 = term if h2 is None else h2 + term
    xhat2, inverse2 = norm_parts(mid[...])
    dmid[...] = ddown_out[...].astype(f32) + norm_back(h2, gain2[...].astype(f32), xhat2, inverse2)
    dbranch_out[...] = dmid[...].astype(bf16)
    wait_weight("o")
    copies = []
    for d in list(range(1, seqs)) + [0]:
        t = ahead[d]
        res = nt(dbranch_out[...], wo[t]).astype(bf16)
        res = res.reshape(batch, cap, res.shape[-1])
        if d == 0:
            recva[0] = res
        else:
            senda[d - 1] = res
            copy = remote(senda.at[d - 1], recva.at[d], sa.at[d - 1], ra.at[d - 1], {"seq": t})
            copy.start()
            copies.append(copy)
    dgain2[...] = jnp.sum(h2 * xhat2, axis=0, keepdims=True)
    dshift2[...] = jnp.sum(h2, axis=0, keepdims=True)
    dbd[...] = jnp.sum(ddown_out[...].astype(f32), axis=0, keepdims=True)
    dbo[...] = jnp.sum(dbranch_out[...].astype(f32), axis=0, keepdims=True)
    for c in range(chunks):
        part = slice(c * size, (c + 1) * size)
        dbu[:, part] = jnp.sum(dhid_out[:, part].astype(f32), axis=0, keepdims=True)
    fetch.wait()
    for copy in copies:
        copy.wait()
    width = qkv.shape[-1] // 3
    heads = width // HD
    lane = lax.broadcasted_iota(jnp.int32, (1, width), 1) // HD
    back = []
    for b in range(batch):
        packed = qkv[:, b].reshape(seqs * cap, 3 * width)
        q, k, v = (packed[:, i * width : (i + 1) * width] for i in range(3))
        q = q * jnp.asarray(HD ** (-0.5), bf16)
        kt = k.T
        da = recva[:, b].reshape(seqs * cap, width)
        live = key_valid(counts, b, cap, behind)
        dk = dv = None
        dqt = []
        for h in range(heads):
            qm = jnp.where(lane == h, q, jnp.zeros_like(q))
            dam = jnp.where(lane == h, da, jnp.zeros_like(da))
            s = jnp.where(live, nt(k, qm), masked_score)
            p = jnp.exp(s - lse[b, h : h + 1, :])
            dp = nt(v, dam)
            inner = jnp.sum(p * dp, axis=0, keepdims=True)
            ds = (p * (dp - inner)).astype(bf16)
            dvh = nn(p.astype(bf16), dam)
            dkh = nn(ds, qm)
            dv = dvh if dv is None else dv + dvh
            dk = dkh if dk is None else dk + dkh
            dqt.append(nn(kt[h * HD : (h + 1) * HD], ds))
        dq = jnp.concatenate(dqt, axis=0).T * HD ** (-0.5)
        grads = jnp.concatenate([dq.astype(bf16), dk.astype(bf16), dv.astype(bf16)], axis=1)
        grads = grads.reshape(seqs, cap, 3 * width)
        recvq[0, b] = grads[0]
        for d in range(1, seqs):
            sendq[d - 1, b] = grads[d]
            copy = remote(
                sendq.at[d - 1, b], recvq.at[d, b], sq.at[d - 1, b], rq.at[d - 1, b], {"seq": behind[d]}
            )
            copy.start()
            back.append(copy)
    x = jnp.where(sec == 0, own[...], got[...]).astype(f32)
    xhat1, inverse1 = norm_parts(x)
    wait_weight("q")
    for copy in back:
        copy.wait()
    h1 = None
    for d in range(seqs):
        t = ahead[d]
        part = recvq[d].reshape(rows, 3 * width)
        dqkv_out[t] = part
        dbqkv[t] = jnp.sum(part.astype(f32), axis=0, keepdims=True)
        term = nt(part, wq[t])
        h1 = term if h1 is None else h1 + term
    dx = dmid[...] + norm_back(h1, gain1[...].astype(f32), xhat1, inverse1)
    dx_out[...] = dx.astype(bf16)
    hop = remote(dx_out, land, ss, rs, {"section": 1 - sec})
    hop.start()
    dgain1[...] = jnp.sum(h1 * xhat1, axis=0, keepdims=True)
    dshift1[...] = jnp.sum(h1, axis=0, keepdims=True)
    hop.wait()
    next_out[...] = land[...]


LINKS = ("x", "yl", "zl", "yh", "zh")


def position():
    f, z = lax.axis_index("fsdp"), lax.axis_index("seq")
    y = lax.div(f, 4)
    c, x = lax.rem(f, 2), lax.rem(lax.div(f, 2), 2)
    yh, zh = lax.div(y, 2), lax.div(z, 2)
    bits = {"c": c, "x": x, "yh": yh, "zh": zh, "yl": lax.rem(y + yh, 2), "zl": lax.rem(z + zh, 2)}
    low = lax.rem(f, 4)
    partner = {
        "c": {"fsdp": f + 1 - 2 * c},
        "x": {"fsdp": f + 2 - 4 * x},
        "yl": {"fsdp": 4 * (y + 1 - 2 * lax.rem(y, 2)) + low},
        "yh": {"fsdp": 4 * (3 - y) + low},
        "zl": {"seq": z + 1 - 2 * lax.rem(z, 2)},
        "zh": {"seq": 3 - z},
    }
    return f, bits, partner


def owner_bits(f):
    y = f // 4
    return {"c": f % 2, "x": (f // 2) % 2, "yh": y // 2, "yl": (y + y // 2) % 2}


def link_of(portion, step):
    return LINKS[(portion + step) % 5]


def piece_of(portion, bits):
    return sum(bits[link_of(portion, s)] << (4 - s) for s in range(5))


def row_groups(start, count):
    row, end = start, start + count
    while row < end:
        portion = min(row // 128, 4)
        size = 32 if portion < 4 else 16
        inner = row - 128 * portion
        take = min(end - row, size - inner % size)
        yield portion, inner // size, inner % size, row - start, take
        row += take


def weight_grad_kernel(
    shape,
    act, ddown, n2, dhid, merged, dbranch, normed, dqkv, dg1, ds1, dbqkv, dbo, dg2, ds2, dbd, dbu,
    gdown, gup, gout, gqkv, og1, os1, obq, obv, obo, og2, os2, obd, obu,
    *scratch,
):
    batch, cap, seqs, shards, chunks = shape
    held, core_in, step_in, final = (scratch[5 * i : 5 * i + 5] for i in range(4))
    vec, vec_in, csem, ssem, zsem, vsem = scratch[20:]
    f, bits, partner = position()
    c = bits["c"]
    greet([partner[n] for n in ("c", "x", "yl", "yh", "zl", "zh")])
    features = ddown.shape[1]
    owned = features // shards

    width = dqkv.shape[2] // 3
    vec[0] = jnp.concatenate(
        [dg1[...], ds1[...]]
        + [jnp.concatenate([dbqkv[t][:, j * width : (j + 1) * width] for t in range(seqs)], axis=1) for j in (0, 2)]
        + [dbo[...], dg2[...], ds2[...], dbd[...]]
        + [dbu[:, j * features : (j + 1) * features] for j in range(chunks)]
        + [jnp.zeros((4, features), f32)],
        axis=0,
    )

    def vec_copy(s):
        name = ("c", "x", "yl", "yh", "zl", "zh")[s]
        return remote(vec.at[s], vec_in.at[s], vsem.at[0, s], vsem.at[1, s], partner[name])

    def vec_step(s):
        copy = vec_copy(s)
        copy.wait()
        vec[s + 1] = vec[s] + vec_in[s]
        if s < 5:
            vec_copy(s + 1).start()

    def put(owner, start, value):
        value = value.astype(bf16)
        own = owner_bits(owner)
        for portion, quarter, inner, at, take in row_groups(start, value.shape[0]):
            place = piece_of(portion, {**own, "zh": quarter // 2, "zl": quarter % 2})
            held[portion][own["c"], place, inner : inner + take] = value[at : at + take]

    def core_copy(i, half):
        b = bits[link_of(i, 0)]
        at = pl.ds(16 * (1 - b if half == 0 else b), 16)
        return remote(
            held[i].at[1 - c, at], core_in[i].at[at], csem.at[0, i, half], csem.at[1, i, half], partner["c"]
        )

    def ready(i):
        core_copy(i, 0).start()
        core_copy(i, 1).start()

    vec_copy(0).start()
    part = lambda j: slice(j * features, (j + 1) * features)
    for j in range(chunks):
        res = tn(act[:, part(j)], ddown[...])
        for k in range(4):
            put(4 * j + k, 0, res[4 * owned * k : 4 * owned * (k + 1)])
    ready(0)
    for j in range(chunks):
        res = tn(n2[...], dhid[:, part(j)])
        for k in range(shards):
            put(k, 192 + owned * j, res[owned * k : owned * (k + 1)])
        if j == 1:
            ready(1)
    ready(2)
    for t in range(seqs):
        res = tn(merged[t], dbranch[...])
        for k in range(4):
            put(4 * t + k, 384, res[owned * k : owned * (k + 1)])
    for j in range(3):
        right = jnp.concatenate([dqkv[t][:, j * width : (j + 1) * width] for t in range(seqs)], axis=1)
        res = tn(normed[...], right)
        for k in range(shards):
            put(k, 432 + owned * j, res[owned * k : owned * (k + 1)])
    ready(3)
    ready(4)

    def add_into(i, base, source, at, count):
        group = min(count, 4)

        def body(k, carry):
            here = pl.ds(base + group * k, group)
            held[i][c, here] = held[i][c, here] + source[pl.ds(at + group * k, group)]
            return carry

        lax.fori_loop(0, count // group, body, 0)

    bases = [0] * 5

    def step_copy(i, s, base):
        name = link_of(i, s)
        half = 16 >> s
        at = 32 - 2 * half
        return remote(
            held[i].at[c, pl.ds(base + (1 - bits[name]) * half, half)],
            step_in[i].at[pl.ds(at, half)],
            ssem.at[0, i, s],
            ssem.at[1, i, s],
            partner[name],
        )

    for i in range(5):
        core_copy(i, 0).wait()
        b = bits[link_of(i, 0)]
        add_into(i, 16 * (1 - b), core_in[i], 16 * (1 - b), 16)
        step_copy(i, 0, 0).start()
    vec_step(0)
    for i in range(5):
        core_copy(i, 1).wait()
        b = bits[link_of(i, 0)]
        add_into(i, 16 * b, core_in[i], 16 * b, 16)
    own_at = []
    for s in range(5):
        for i in range(5):
            half = 16 >> s
            copy = step_copy(i, s, bases[i])
            bases[i] = bases[i] + bits[link_of(i, s)] * half
            copy.wait()
            add_into(i, bases[i], step_in[i], 32 - 2 * half, half)
            if s < 4:
                step_copy(i, s + 1, bases[i]).start()
        vec_step(s + 1)

    def z_copy(i, s):
        first, second = ("zl", "zh") if i % 2 == 0 else ("zh", "zl")
        if s == 0:
            at, to = pl.ds(2 * bits[second] + bits[first], 1), partner[first]
        else:
            at, to = pl.ds(2 * bits[second], 2), partner[second]
        return remote(final[i].at[at], final[i].at[at], zsem.at[0, i, s], zsem.at[1, i, s], to)

    for i in range(5):
        first, second = ("zl", "zh") if i % 2 == 0 else ("zh", "zl")
        final[i][2 * bits[second] + bits[first]] = held[i][c, bases[i]]
        z_copy(i, 0).start()
    for i in range(5):
        z_copy(i, 0).wait()
        z_copy(i, 1).start()
    total = vec[6]
    mine = pltpu.roll(total, lax.rem(features - f * owned, features), 1)
    for r, out in enumerate((og1, os1, obq, obv, obo, og2, os2, obd)):
        out[...] = mine[r : r + 1, :owned]
    wide = 4 * owned
    quarter = pltpu.roll(total, lax.rem(features - lax.rem(f, 4) * wide, features), 1)
    chosen = lax.broadcasted_iota(jnp.int32, (16, 1), 0) == 8 + lax.div(f, 4)
    obu[...] = jnp.sum(jnp.where(chosen, quarter, 0.0), axis=0, keepdims=True)[:, :wide]
    for i in range(5):
        z_copy(i, 1).wait()

    def share(start, count):
        got = []
        for portion, quarter, inner, _, take in row_groups(start, count):
            zh, zl = quarter // 2, quarter % 2
            place = 2 * zh + zl if portion % 2 == 0 else 2 * zl + zh
            got.append(final[portion][place, inner : inner + take])
        return jnp.concatenate(got, axis=0)

    gdown[...] = share(0, 4 * owned)
    for j in range(chunks):
        gup[:, part(j)] = share(192 + owned * j, owned)
    gout[...] = share(384, owned)
    for j in range(3):
        gqkv[:, part(j)] = share(432 + owned * j, owned)


def per_device(
    images_in, counts, cotangent, gain_one, shift_one, w_qkv, bias_query, bias_value, w_out,
    bias_out, gain_two, shift_two, w_up, bias_up, w_down, bias_down,
):
    micro, images, cap, features = images_in.shape
    batch = micro * images
    seqs = lax.axis_size("seq")
    shards = lax.axis_size("fsdp")
    rows = batch * cap
    width = features // seqs
    owned = features // shards
    ff = w_up.shape[-1]
    chunks = ff // features

    def blocks_of(columns):
        return columns.reshape(-1, 3, seqs, width).transpose(2, 0, 1, 3).reshape(seqs, -1, 3 * width)

    def gathered(a):
        return lax.all_gather(a, "fsdp", axis=0, tiled=True)

    small = jnp.concatenate(
        [gain_one[0], shift_one[0], bias_query[0], bias_value[0], bias_out[0], gain_two[0],
         shift_two[0], bias_down[0], bias_up[0]]
    )
    small = lax.all_gather(small, "fsdp", axis=0, tiled=False)
    vec = [small[:, i * owned : (i + 1) * owned].reshape(1, features) for i in range(8)]
    g1, s1, bq, bv, bo, g2, s2, bd = vec
    bu = small[:, 8 * owned :].reshape(1, ff)
    bqkv = jnp.concatenate([bq, jnp.zeros_like(bq), bv], axis=1)
    bqkv = blocks_of(bqkv)
    wq_h = lax.all_gather(blocks_of(w_qkv[0]), "fsdp", axis=0, tiled=False)
    wo_h = gathered(w_out[0]).reshape(seqs, width, features)
    wu_h = gathered(w_up[0])
    wd_h = gathered(w_down[0])

    own = images_in.reshape(rows, features)
    cot = cotangent.reshape(rows, features)
    table = counts.reshape(batch, seqs)
    shape = (batch, cap, seqs, shards, chunks)
    vmem = pl.BlockSpec(memory_space=pltpu.VMEM)
    smem = pl.BlockSpec(memory_space=pltpu.SMEM)
    hbm = pl.BlockSpec(memory_space=pl.ANY)
    weight_scratch = [
        pltpu.VMEM((seqs, features, 3 * width), bf16),
        pltpu.VMEM((seqs, width, features), bf16),
        pltpu.VMEM((features, ff), bf16),
        pltpu.VMEM((ff, features), bf16),
    ]
    dma = pltpu.SemaphoreType.DMA
    sds = jax.ShapeDtypeStruct

    def forward(got):
        return pl.pallas_call(
            functools.partial(forward_kernel, shape),
            name="forward_stage",
            out_shape=(
                sds((rows, features), bf16),
                sds((rows, features), bf16),
                sds((seqs, batch, cap, 3 * width), bf16),
                sds((batch, 8, seqs * cap), f32),
                sds((rows, features), bf16),
                sds((rows, features), f32),
                sds((seqs, rows, width), bf16),
                sds((rows, features), bf16),
                sds((rows, ff), bf16),
                sds((rows, ff), bf16),
            ),
            in_specs=[smem] + [vmem] * 10 + [hbm] * 4,
            out_specs=[vmem, vmem, hbm] + [vmem] * 7,
            scratch_shapes=weight_scratch
            + [
                pltpu.VMEM((seqs - 1, batch, cap, 3 * width), bf16),
                pltpu.VMEM((seqs, batch, cap, 3 * width), bf16),
                pltpu.VMEM((seqs - 1, batch, cap, width), bf16),
                pltpu.VMEM((seqs, batch, cap, width), bf16),
                pltpu.VMEM((rows, features), bf16),
                dma((5,)),
                dma((seqs - 1,)),
                dma((seqs - 1,)),
                dma((seqs - 1, batch)),
                dma((seqs - 1, batch)),
                dma,
                dma,
            ],
            compiler_params=pltpu.CompilerParams(
                collective_id=0, has_side_effects=True, vmem_limit_bytes=VMEM_LIMIT
            ),
        )(table, own, got, g1, s1, bqkv, bo, g2, s2, bu, bd, wq_h, wo_h, wu_h, wd_h)

    def backward(got, ggot, stash):
        qkv, lse, normed, mid, act, slope = stash
        vector = sds((1, features), f32)
        return pl.pallas_call(
            functools.partial(backward_kernel, shape),
            name="backward_stage",
            out_shape=(
                sds((rows, features), bf16),
                sds((rows, features), bf16),
                sds((rows, features), bf16),
                sds((rows, ff), bf16),
                sds((rows, features), bf16),
                sds((seqs, rows, 3 * width), bf16),
                vector,
                vector,
                sds((seqs, 1, 3 * width), f32),
                vector,
                vector,
                vector,
                sds((1, ff), f32),
                vector,
            ),
            in_specs=[smem] + [vmem] * 11 + [hbm] * 5,
            out_specs=[vmem] * 14,
            scratch_shapes=weight_scratch
            + [
                pltpu.VMEM((seqs, batch, cap, 3 * width), bf16),
                pltpu.VMEM((seqs - 1, batch, cap, width), bf16),
                pltpu.VMEM((seqs, batch, cap, width), bf16),
                pltpu.VMEM((seqs - 1, batch, cap, 3 * width), bf16),
                pltpu.VMEM((seqs, batch, cap, 3 * width), bf16),
                pltpu.VMEM((rows, features), bf16),
                pltpu.VMEM((rows, features), f32),
                dma((5,)),
                dma((seqs - 1,)),
                dma((seqs - 1,)),
                dma((seqs - 1, batch)),
                dma((seqs - 1, batch)),
                dma,
                dma,
            ],
            compiler_params=pltpu.CompilerParams(
                collective_id=1, has_side_effects=True, vmem_limit_bytes=VMEM_LIMIT
            ),
        )(table, own, got, cot, ggot, lse, normed, mid, act, slope, g1, g2, qkv, wq_h, wo_h, wu_h, wd_h)

    first = forward(own)
    y, _, qkv, lse, normed, mid, merged, n2, act, slope = forward(first[1])
    stash = (qkv, lse, normed, mid, act, slope)
    early = backward(first[1], cot, stash)
    dx, _, ddown, dhid, dbranch, dqkv, dg1, ds1, dbqkv, dbo, dg2, ds2, dbu, dbd = backward(
        first[1], early[1], stash
    )

    sizes = (32, 32, 32, 32, 16)
    vector = sds((1, owned), f32)
    grads = pl.pallas_call(
        functools.partial(weight_grad_kernel, shape),
        name="weight_gradients",
        out_shape=(
            sds((4 * owned, features), bf16),
            sds((owned, ff), bf16),
            sds((owned, features), bf16),
            sds((owned, 3 * features), bf16),
            *([vector] * 8),
            sds((1, 4 * owned), f32),
        ),
        in_specs=[vmem] * 16,
        out_specs=[vmem] * 13,
        scratch_shapes=[pltpu.VMEM((2, 32, r, features), bf16) for r in sizes]
        + [pltpu.VMEM((32, r, features), bf16) for r in sizes]
        + [pltpu.VMEM((32, r, features), bf16) for r in sizes]
        + [pltpu.VMEM((4, r, features), bf16) for r in sizes]
        + [
            pltpu.VMEM((7, 16, features), f32),
            pltpu.VMEM((6, 16, features), f32),
            dma((2, 5, 2)),
            dma((2, 5, 5)),
            dma((2, 5, 2)),
            dma((2, 6)),
        ],
        compiler_params=pltpu.CompilerParams(
            collective_id=2, has_side_effects=True, vmem_limit_bytes=VMEM_LIMIT
        ),
    )(act, ddown, n2, dhid, merged, dbranch, normed, dqkv, dg1, ds1, dbqkv, dbo, dg2, ds2, dbd, dbu)
    gw_down, gw_up, gw_out, gw_qkv = (g.astype(f32)[None] for g in grads[:4])
    gg1, gs1, gbq, gbv, gbo, gg2, gs2, gbd, gbu = grads[4:]
    out_shape = (1, micro, images, cap, features)
    return (
        y.reshape(out_shape), dx.reshape(out_shape), gg1, gs1, gw_qkv, gbq, gbv, gw_out, gbo, gg2, gs2,
        gw_up, gbu, gw_down, gbd,
    )


def solution(mesh):
    token = P(None, "fsdp", "seq", None)
    vector = P("section", "fsdp")
    matrix = P("section", "fsdp", None)
    result = P("section", None, "fsdp", "seq", None)
    return jax.shard_map(
        per_device,
        mesh=mesh,
        in_specs=(
            token, P(None, "fsdp", None), token, vector, vector, matrix, vector, vector, matrix, vector,
            vector, vector, matrix, vector, matrix, vector,
        ),
        out_specs=(
            result, result, vector, vector, matrix, vector, vector, matrix, vector, vector, vector,
            matrix, vector, matrix, vector,
        ),
        check_vma=False,
    )
```

time: 917 us -> 509 us (0.56)
  Pallas kernels: 0 us -> 314 us
  waiting for transfers between devices: 297 us -> 91.5 us
  matrix products: 197 us -> 0 us
  local copies, waits for them, and re-layouts: 203 us -> 15.4 us
  other arithmetic: 89.9 us -> 6.15 us
  starting transfers between devices: 64.1 us -> 0.16 us
  blocking collectives: 39.8 us -> 56.2 us
    pallas_call x0 -> x5, Pallas kernels: none -> 314 us  [the longest x2 125 us: backward(): pl.pallas_call(functools.partial(backward_kernel, shape), name='backward_...]
    dot_general x57 -> x0, matrix products: 197 us -> none  [the longest x12 65.3 us: contract_rows(): lax.dot_general(left, right, (((0,), (0,)), ((), ())), preferred_element_...]
    reduce_scatter x1 -> x0, waiting for transfers between devices: 102 us -> none  [sent_together(): lax.psum_scatter(both, axis, scatter_dimension=dim, tiled=True)]
    unnamed x384 -> x58, local copies, waits for them, and re-layouts: 78.7 us -> 7.13 us
    all_to_all x12 -> x0, starting transfers between devices: 49.6 us -> none  [the longest x3 13.5 us: layer_backward(): lax.all_to_all(grad_triples, 'seq', split_axis=1, concat_axis=3, tiled=True)]
    unnamed x8 -> x4, waiting for transfers between devices: 48.8 us -> 1.9 us
    all_to_all x12 -> x0, waiting for transfers between devices: 39.4 us -> none  [the longest x3 24.4 us: layer_forward(): lax.all_to_all(triples, 'seq', split_axis=3, concat_axis=1, tiled=True)]
    all_gather x2 -> x4, waiting for transfers between devices: 57.4 us -> 89.6 us  [the longest x3 80.6 us: gathered(): return lax.all_gather(a, 'fsdp', axis=0, tiled=True)]
  transfers between devices with their start and end apart: 22 -> 4, of which waited for: 16 -> 3; matrix products, arithmetic and copies ran while one was open for 25% -> 2% of each run, Pallas kernels for 0% -> 0%
where the time goes in v1:
time: 509 us; the launch traced here: 499 us
  Pallas kernels  314 us (62%)
  waiting for transfers between devices  91.5 us (18%)
  blocking collectives  56.2 us (11%)
  local copies, waits for them, and re-layouts  15.4 us (3%)
  between operations  14.9 us (3%)
  other arithmetic  6.15 us (1%)
    pallas_call x2, Pallas kernels, backward(): pl.pallas_call(functools.partial(backward_kernel, shape), name='backward_...  125 us
    pallas_call x2, Pallas kernels, forward(): pl.pallas_call(functools.partial(forward_kernel, shape), name='forward_st...  118 us
    all_gather x3, waiting for transfers between devices, gathered(): return lax.all_gather(a, 'fsdp', axis=0, tiled=True)  80.6 us
    pallas_call x1, Pallas kernels, per_device(): pl.pallas_call(functools.partial(weight_grad_kernel, shape), name='weight...  70.7 us
    unnamed x1, blocking collectives  56.2 us
  transfers between devices with their start and end apart: 4, of which 3 were waited for; matrix products, arithmetic and copies ran while one was open for 2% of the time, Pallas kernels for 0%

profile of v1, /device:TPU:0, one launch (start us, length us, event | category | flops | bytes accessed | tf_op | source)
XLA Modules:
  0.0 498.8 jit_solution(6108419665889141952)
XLA Ops:
  7.3 0.7 all-gather.11.cloned.1.call-update
  8.1 1.2 reshape_squeeze.3
  9.5 1.0 all_gather_reshape.3
  10.5 0.7 all-gather.13.cloned.1.call-update
  11.3 0.5 all-gather.15.cloned.1.call-update
  11.8 0.6 dynamic-slice
  13.5 56.2 %all-reduce = bf16[9216]{0:T(1024)(128)(2,1)S(1)} all-reduce(bf16[9216]{0:T(1024)(128)(2,1)S(1)} %dynamic-update-slice), channel_id=2, replica_groups=mesh['section'=2,'seq'=4,'fsdp'=16] {'fsdp'}, use_global_device_ids=true, to_apply=%add | all-reduce | flops 9216 | bytes 36864
  69.9 0.7 reshape.88.bu
  70.6 0.7 reshape.89.bd
  71.6 0.7 reshape.108.bqkv
  72.3 0.7 reshape.86.gain2
  73.0 0.7 reshape.82.gain1
  73.6 0.7 reshape.87.shift2
  74.3 0.7 reshape.85.bo
  75.0 0.7 reshape.83.shift1
  75.7 9.0 %all-gather.9.cloned.1.call-done.wq_h = bf16[16,4,48,576]{3,2,1,0:T(8,128)(2,1)} async-done(((bf16[1,4,48,576]{3,2,1,0:T(8,128)(2,1)}), bf16[16,4,48,576]{3,2,1,0:T(8,128)(2,1)}) %all-gather.9.cloned.1.call-update) | async-done | bytes 3538960 | tf_op jit(solution)/shard_map/all_gather | solution.py:564
  84.7 40.4 %all-gather.13.cloned.1.call-done = bf16[1,768,3072]{2,1,0:T(8,128)(2,1)} async-done(((bf16[1,48,3072]{2,1,0:T(8,128)(2,1)}), bf16[1,768,3072]{2,1,0:T(8,128)(2,1)}) %all-gather.13.cloned.1.call-update) | async-done | bytes 4718608 | tf_op jit(solution)/shard_map/all_gather | solution.py:552
  125.1 40.2 %all-gather.15.cloned.1.call-done = bf16[1,3072,768]{2,1,0:T(8,128)(2,1)} async-done(((bf16[1,192,768]{2,1,0:T(8,128)(2,1)}), bf16[1,3072,768]{2,1,0:T(8,128)(2,1)}) %all-gather.15.cloned.1.call-update) | async-done | bytes 4718608 | tf_op jit(solution)/shard_map/all_gather | solution.py:552
  165.3 61.5 %forward_stage.2 = (bf16[320,768]{1,0:T(8,128)(2,1)}, bf16[320,768]{1,0:T(8,128)(2,1)}, bf16[4,2,160,576]{3,2,1,0:T(8,128)(2,1)}, f32[2,8,640]{2,1,0:T(8,128)}, ...) custom-call(s32[2,4]{1,0:T(2,128)} %bitcast.64, ...), custom_call_target="tpu_custom_call" | custom-call | tf_op jit(solution)/shard_map/forward_stage/pallas_call | solution.py:586
  226.8 56.8 %forward_stage.3 = (bf16[320,768]{1,0:T(8,128)(2,1)}, bf16[320,768]{1,0:T(8,128)(2,1)}, bf16[4,2,160,576]{3,2,1,0:T(8,128)(2,1)}, f32[2,8,640]{2,1,0:T(8,128)}, ...) custom-call(s32[2,4]{1,0:T(2,128)} %bitcast.65, ...), custom_call_target="tpu_custom_call" | custom-call | tf_op jit(solution)/shard_map/forward_stage/pallas_call | solution.py:586
  283.6 62.7 %backward_stage.2 = (bf16[320,768]{1,0:T(8,128)(2,1)}, bf16[320,768]{1,0:T(8,128)(2,1)}, bf16[320,768]{1,0:T(8,128)(2,1)}, bf16[320,3072]{1,0:T(8,128)(2,1)}, bf...) custom-call(s32[2,4]{1,0:T(2,128)} %bitcast.66, ...), custom_call_target="tpu_custom_call" | custom-call | tf_op jit(solution)/shard_map/backward_stage/pallas_call | solution.py:626
  346.3 62.7 %backward_stage.3 = (bf16[320,768]{1,0:T(8,128)(2,1)}, bf16[320,768]{1,0:T(8,128)(2,1)}, bf16[320,768]{1,0:T(8,128)(2,1)}, bf16[320,3072]{1,0:T(8,128)(2,1)}, bf...) custom-call(s32[2,4]{1,0:T(2,128)} %bitcast.67, ...), custom_call_target="tpu_custom_call" | custom-call | tf_op jit(solution)/shard_map/backward_stage/pallas_call | solution.py:626
  409.0 70.7 %weight_gradients.1 = (bf16[192,768]{1,0:T(8,128)(2,1)}, bf16[48,3072]{1,0:T(8,128)(2,1)}, bf16[48,768]{1,0:T(8,128)(2,1)}, bf16[48,2304]{1,0:T(8,128)(2,1)}, f3...) custom-call(bf16[320,3072]{1,0:T(8,128)(2,1)} %get-tuple-element.57., ...), custom_call_target="tpu_custom_call" | custom-call | tf_op jit(solution)/shard_map/weight_gradients/pallas_call | solution.py:679
  479.7 1.7 bitcast_convert_fusion.3
  481.3 1.7 bitcast_convert_fusion.2
  483.1 1.8 bitcast_convert_fusion.1
  485.0 0.9 bitcast_convert_fusion
  485.8 0.8 copy.67
  486.6 0.8 copy.68
  487.4 0.5 copy.69
  488.4 0.5 copy.71
  491.0 0.6 copy.76
  (69 shorter events, 4.4 us)
Async XLA Ops:
  7.2 4.6 copy-start.21
  7.2 5.9 %copy-start.3 = (bf16[1,192]{1,0:T(2,128)(2,1)S(1)}, bf16[1,192]{1,0:T(2,128)(2,1)}, u32[]{:S(2)}) copy-start(bf16[1,192]{1,0:T(2,128)(2,1)} %param.29) | copy-start | bytes 1156
  7.2 5.9 %copy-start.12 = (bf16[1,48]{1,0:T(2,128)(2,1)S(1)}, bf16[1,48]{1,0:T(2,128)(2,1)}, u32[]{:S(2)}) copy-start(bf16[1,48]{1,0:T(2,128)(2,1)} %param.31) | copy-start | bytes 292
  7.2 5.9 %copy-start.11 = (bf16[1,48]{1,0:T(2,128)(2,1)S(1)}, bf16[1,48]{1,0:T(2,128)(2,1)}, u32[]{:S(2)}) copy-start(bf16[1,48]{1,0:T(2,128)(2,1)} %param.27) | copy-start | bytes 292
  7.2 5.9 %copy-start.10 = (bf16[1,48]{1,0:T(2,128)(2,1)S(1)}, bf16[1,48]{1,0:T(2,128)(2,1)}, u32[]{:S(2)}) copy-start(bf16[1,48]{1,0:T(2,128)(2,1)} %param.26) | copy-start | bytes 292
  7.2 5.9 %copy-start.9 = (bf16[1,48]{1,0:T(2,128)(2,1)S(1)}, bf16[1,48]{1,0:T(2,128)(2,1)}, u32[]{:S(2)}) copy-start(bf16[1,48]{1,0:T(2,128)(2,1)} %param.25) | copy-start | bytes 292
  7.2 5.9 %copy-start.8 = (bf16[1,48]{1,0:T(2,128)(2,1)S(1)}, bf16[1,48]{1,0:T(2,128)(2,1)}, u32[]{:S(2)}) copy-start(bf16[1,48]{1,0:T(2,128)(2,1)} %param.23) | copy-start | bytes 292
  7.3 5.9 %copy-start.7 = (bf16[1,48]{1,0:T(2,128)(2,1)S(1)}, bf16[1,48]{1,0:T(2,128)(2,1)}, u32[]{:S(2)}) copy-start(bf16[1,48]{1,0:T(2,128)(2,1)} %param.22) | copy-start | bytes 292
  7.3 5.9 %copy-start.6 = (bf16[1,48]{1,0:T(2,128)(2,1)S(1)}, bf16[1,48]{1,0:T(2,128)(2,1)}, u32[]{:S(2)}) copy-start(bf16[1,48]{1,0:T(2,128)(2,1)} %param.20) | copy-start | bytes 292
  7.3 5.9 %copy-start.5 = (bf16[1,48]{1,0:T(2,128)(2,1)S(1)}, bf16[1,48]{1,0:T(2,128)(2,1)}, u32[]{:S(2)}) copy-start(bf16[1,48]{1,0:T(2,128)(2,1)} %param.19) | copy-start | bytes 292
  7.3 68.4 %all-gather.11.cloned.1.call-start = ((), (), s32[]{:S(2)}) async-start(), calls=%async_computation.1 | async-start | bytes 1253376 | tf_op jit(solution)/shard_map/all_gather | solution.py:552
  8.0 76.6 %all-gather.9.cloned.1.call-start = ((), (), s32[]{:S(2)}) async-start(), calls=%async_computation | async-start | bytes 4177920 | tf_op jit(solution)/shard_map/all_gather | solution.py:564
  10.5 114.6 %all-gather.13.cloned.1.call-start = ((), (), s32[]{:S(2)}) async-start(), calls=%async_computation.2 | async-start | bytes 5013504 | tf_op jit(solution)/shard_map/all_gather | solution.py:552
  11.2 154.0 %all-gather.15.cloned.1.call-start = ((), (), s32[]{:S(2)}) async-start(), calls=%async_computation.3 | async-start | bytes 5013504 | tf_op jit(solution)/shard_map/all_gather | solution.py:552
  479.7 5.3 %copy-start.2 = (bf16[192,768]{1,0:T(8,128)(2,1)S(1)}, bf16[192,768]{1,0:T(8,128)(2,1)}, u32[]{:S(2)}) copy-start(bf16[192,768]{1,0:T(8,128)(2,1)} %get-tuple-element.87) | copy-start | bytes 884740
  479.7 6.1 %copy-start = (bf16[320,768]{1,0:T(8,128)(2,1)S(1)}, bf16[320,768]{1,0:T(8,128)(2,1)}, u32[]{:S(2)}) copy-start(bf16[320,768]{1,0:T(8,128)(2,1)} %get-tuple-element.53) | copy-start | bytes 1474564
  479.7 6.9 %copy-start.1 = (bf16[320,768]{1,0:T(8,128)(2,1)S(1)}, bf16[320,768]{1,0:T(8,128)(2,1)}, u32[]{:S(2)}) copy-start(bf16[320,768]{1,0:T(8,128)(2,1)} %get-tuple-element.61) | copy-start | bytes 1474564
  483.1 4.3 copy-start.20
  483.1 4.8 copy-start.19
  483.1 5.3 %copy-start.18 = (f32[1,48]{1,0:T(1,128)S(1)}, f32[1,48]{1,0:T(1,128)}, u32[]{:S(2)}) copy-start(f32[1,48]{1,0:T(1,128)} %get-tuple-element.177) | copy-start | bytes 580
  483.1 5.8 %copy-start.17 = (f32[1,48]{1,0:T(1,128)S(1)}, f32[1,48]{1,0:T(1,128)}, u32[]{:S(2)}) copy-start(f32[1,48]{1,0:T(1,128)} %get-tuple-element.178) | copy-start | bytes 580
  483.1 6.3 %copy-start.16 = (f32[1,48]{1,0:T(1,128)S(1)}, f32[1,48]{1,0:T(1,128)}, u32[]{:S(2)}) copy-start(f32[1,48]{1,0:T(1,128)} %get-tuple-element.180) | copy-start | bytes 580
  483.1 6.8 %copy-start.15 = (f32[1,48]{1,0:T(1,128)S(1)}, f32[1,48]{1,0:T(1,128)}, u32[]{:S(2)}) copy-start(f32[1,48]{1,0:T(1,128)} %get-tuple-element.181) | copy-start | bytes 580
  483.1 7.4 %copy-start.14 = (f32[1,48]{1,0:T(1,128)S(1)}, f32[1,48]{1,0:T(1,128)}, u32[]{:S(2)}) copy-start(f32[1,48]{1,0:T(1,128)} %get-tuple-element.182) | copy-start | bytes 580
  483.1 7.9 %copy-start.4 = (f32[1,192]{1,0:T(1,128)S(1)}, f32[1,192]{1,0:T(1,128)}, u32[]{:S(2)}) copy-start(f32[1,192]{1,0:T(1,128)} %get-tuple-element.184) | copy-start | bytes 2308
  483.1 8.4 %copy-start.13 = (f32[1,48]{1,0:T(1,128)S(1)}, f32[1,48]{1,0:T(1,128)}, u32[]{:S(2)}) copy-start(f32[1,48]{1,0:T(1,128)} %get-tuple-element.186) | copy-start | bytes 580
Sparse Core Ops, SparseCore 0:
  9.8 35.1 all-gather.10
  47.3 37.2 all-gather.8
  86.4 38.6 all-gather.12
  126.6 38.5 all-gather.14
